TPU v7x, 512 devices: a whole 4x8x8 slice. The times are simulated.
512 devices in a mesh: exp: 64 (over x, y, core), et: 8 (over z).
Axes of the slice: x: 4, y: 8, z: 8, core: 2. Of those that a mesh axis runs over, the one named last changes fastest.
Arguments:
- out_grad: bfloat16 [4096, 2048], P('exp', 'et'), may hold values from -1.5 to 1.5
- gate_scores: float32 [4096, 8], P('exp'), may hold values from 0.1 to 1
- expert_ids: int32 [4096, 8], P('exp'), may hold values from 0 to 63, all different within a row; in each aligned block of 64 rows (0 to 63, 64 to 127, ...) at most 16 rows name the same one
- routed_rows: bfloat16 [64, 1024, 2048], P('exp', None, 'et'), may hold values from -6 to 6
- gate_pre: bfloat16 [64, 768, 1024], P('exp', 'et'), may hold values from -6 to 6
- up_pre: bfloat16 [64, 768, 1024], P('exp', 'et'), may hold values from -6 to 6
- gate_weight: bfloat16 [64, 768, 2048], P('exp', 'et'), may hold values from -0.125 to 0.125
- up_weight: bfloat16 [64, 768, 2048], P('exp', 'et'), may hold values from -0.125 to 0.125
- down_weight: bfloat16 [64, 768, 2048], P('exp', 'et'), may hold values from -0.21875 to 0.21875
Outputs:
- token_grad: bfloat16 [4096, 2048], P('exp', 'et')
- score_grad: float32 [4096, 8], P('exp')
- gate_weight_grad: bfloat16 [64, 768, 2048], P('exp', 'et')
- up_weight_grad: bfloat16 [64, 768, 2048], P('exp', 'et')
- down_weight_grad: bfloat16 [64, 768, 2048], P('exp', 'et')
Inputs may be any that keep to these rules, and one draw needn't show every extreme that they name: `expert_ids`: within each block of 64 tokens (the tokens of one index of exp) no expert is named more than 16 times, and in every draw some block names some expert exactly 16 times; each token names 8 different experts.
All inputs are finite; a program needn't handle non-finite values.
Results may differ from a plain program's by a relative error of at most 0.018.
Values may be sent and summed in bfloat16 or wider, within the bound.
A program may use at most 64 MiB of HBM per device.

v0:
```python
import jax
import jax.numpy as jnp
from jax import lax
from jax.sharding import PartitionSpec as P


def to_slots(received):
    moved = jnp.moveaxis(received, 0, 1)
    return moved.reshape((moved.shape[0], moved.shape[1] * moved.shape[2]) + moved.shape[3:])


def from_slots(local, exp_count):
    shaped = local.reshape(
        (local.shape[0], exp_count, local.shape[1] // exp_count) + local.shape[2:]
    )
    return jnp.moveaxis(shaped, 1, 0)


def body(
    out_grad,
    gate_scores,
    expert_ids,
    routed_rows,
    gate_pre,
    up_pre,
    gate_weight,
    up_weight,
    down_weight,
):
    exp_count = lax.axis_size("exp")
    local_experts = routed_rows.shape[0]
    slot_count = routed_rows.shape[1]
    most_rows = slot_count // exp_count
    expert_count = local_experts * exp_count
    tok_count = expert_ids.shape[0]
    top_count = expert_ids.shape[1]
    ids_flat = expert_ids.reshape(-1)
    labels = jnp.arange(expert_count, dtype=jnp.int32)
    onehot = (ids_flat[:, None] == labels[None, :]).astype(jnp.int32)
    slot_rank = jnp.sum((jnp.cumsum(onehot, axis=0) - onehot) * onehot, axis=1)
    slot_send = ids_flat * most_rows + slot_rank
    score_send = (
        jnp.zeros((expert_count * most_rows,), jnp.float32)
        .at[slot_send]
        .set(gate_scores.reshape(-1))
    )
    score_send = score_send.reshape(exp_count, local_experts, most_rows)
    whole_grad = lax.all_gather(out_grad, "et", axis=1, tiled=True)
    repeated = jnp.repeat(whole_grad, top_count, axis=0)
    buffer = (
        jnp.zeros((expert_count * most_rows, whole_grad.shape[1]), jnp.bfloat16)
        .at[slot_send]
        .set(repeated)
    )
    got_rows = lax.all_to_all(
        buffer.reshape(exp_count, local_experts, most_rows, whole_grad.shape[1]),
        "exp",
        split_axis=0,
        concat_axis=0,
        tiled=True,
    )
    got_scores = lax.all_to_all(
        score_send.astype(jnp.bfloat16), "exp", split_axis=0, concat_axis=0, tiled=True
    ).astype(score_send.dtype)
    row_grad = to_slots(got_rows)
    row_score = to_slots(got_scores)
    gate_cols, up_cols = (
        lax.all_to_all(gate_weight, "et", split_axis=2, concat_axis=1, tiled=True),
        lax.all_to_all(up_weight, "et", split_axis=2, concat_axis=1, tiled=True),
    )
    hidden_raw = jnp.einsum(
        "efd,esd->efs", down_weight, row_grad, preferred_element_type=jnp.float32
    )
    gate_val = gate_pre.astype(jnp.float32)
    up_val = up_pre.astype(jnp.float32)
    sigma = jax.nn.sigmoid(gate_val)
    silu_val = gate_val * sigma
    hidden = (silu_val * up_val).astype(jnp.bfloat16)
    score_local = jnp.sum(hidden.astype(jnp.float32) * hidden_raw, axis=1)
    score_total = lax.psum(score_local, "et")
    hidden_grad = row_score[:, None, :] * hidden_raw
    gate_grad = (hidden_grad * up_val * sigma * (1.0 + gate_val * (1.0 - sigma))).astype(
        jnp.bfloat16
    )
    up_grad = (hidden_grad * silu_val).astype(jnp.bfloat16)
    scaled_grad = (row_score[:, :, None] * row_grad.astype(jnp.float32)).astype(jnp.bfloat16)
    down_out = jnp.einsum(
        "efs,esd->efd", hidden, scaled_grad, preferred_element_type=jnp.float32
    ).astype(jnp.bfloat16)
    gate_every, up_every = (
        lax.all_gather(gate_grad, "et", axis=1, tiled=True),
        lax.all_gather(up_grad, "et", axis=1, tiled=True),
    )
    input_rows = jnp.einsum(
        "efs,efd->esd", gate_every, gate_cols, preferred_element_type=jnp.float32
    )
    input_rows = input_rows + jnp.einsum(
        "efs,efd->esd", up_every, up_cols, preferred_element_type=jnp.float32
    )
    input_rows = input_rows.astype(jnp.bfloat16)
    piece_rows = lax.all_gather(routed_rows, "et", axis=2, tiled=True)
    gate_piece = jnp.einsum(
        "efs,esp->efp", gate_grad, piece_rows, preferred_element_type=jnp.float32
    )
    up_piece = jnp.einsum("efs,esp->efp", up_grad, piece_rows, preferred_element_type=jnp.float32)
    both_grads = jnp.stack([gate_piece, up_piece]).astype(jnp.bfloat16)
    gate_out = both_grads[0]
    up_out = both_grads[1]
    back_rows, back_scores = (
        lax.all_to_all(
            from_slots(input_rows, exp_count), "exp", split_axis=0, concat_axis=0, tiled=True
        ),
        lax.all_to_all(
            from_slots(score_total, exp_count).astype(jnp.bfloat16),
            "exp",
            split_axis=0,
            concat_axis=0,
            tiled=True,
        ).astype(jnp.float32),
    )
    back_rows = back_rows.reshape(expert_count * most_rows, back_rows.shape[3])
    picked = back_rows[slot_send].reshape(tok_count, top_count, back_rows.shape[1])
    token_grad = jnp.sum(picked.astype(jnp.float32), axis=1).astype(jnp.bfloat16)
    score_grad = back_scores.reshape(-1)[slot_send].reshape(tok_count, top_count)
    return (token_grad, score_grad, gate_out, up_out, down_out)


def solution(mesh):
    return jax.shard_map(
        body,
        mesh=mesh,
        in_specs=(
            P("exp", "et"),
            P("exp", None),
            P("exp", None),
            P("exp", None, "et"),
            P("exp", "et", None),
            P("exp", "et", None),
            P("exp", "et", None),
            P("exp", "et", None),
            P("exp", "et", None),
        ),
        out_specs=(
            P("exp", "et"),
            P("exp", None),
            P("exp", "et", None),
            P("exp", "et", None),
            P("exp", "et", None),
        ),
        check_vma=False,
    )
```

profile of v0, /device:TPU:1, one launch (start us, length us, event | category | flops | bytes accessed | tf_op | source)
XLA Modules:
  0.0 347.6 jit_solution(15882865796638221119)
XLA Ops:
  7.2 0.8 copy.29
  8.2 0.7 broadcast_multiply_fusion
  8.9 1.2 reduce-window.6
  10.1 0.2 slice_reduce_fusion
  10.5 0.1 mul.84
  10.6 0.8 copy.32
  11.4 0.1 fusion.58
  11.6 2.4 scatter_custom_fusion
  14.0 0.7 convert_element_type.139
  14.7 11.6 %all-to-all-start = ((bf16[64,1,16]{2,1,0:T(2,128)(2,1)}), bf16[64,1,16]{2,1,0:T(2,128)(2,1)S(1)}, u32[]{:S(2)}, u32[]{:S(2)}) async-start(bf16[64,1,16]{2,1,0:T(2,128)(2,1)} %convert_element_type.139), calls=%async_computation | async-start | bytes 65536 | tf_op jit(solution)/shard_map/all_to_all | solution.py:62
  26.3 25.3 %all_gather.12 = bf16[64,2048]{1,0:T(8,128)(2,1)S(1)} all-gather(bf16[64,256]{1,0:T(8,128)(2,1)} %param.9), channel_id=1, replica_groups=mesh['exp'=64,'et'=8] {'et'}, dimensions={1}, use_global_device_ids=true | all-gather | bytes 294912 | tf_op jit(solution)/shard_map/all_gather | solution.py:48
  51.6 6.2 %scatter_custom_fusion.1 = bf16[1024,2048]{1,0:T(8,128)(2,1)} fusion(s32[512]{0:T(512)S(1)} %bitcast.140, bf16[]{:T(256)} %constant.5.clone.1, bf16[64,2048]{1,0:T(8,128)(2,1)S(1)} %all_gather.12), kind=kCustom, calls=%fused_computation.19 | custom fusion | bytes 4456450 | tf_op jit(solution)/shard_map/scatter | solution.py:53
  57.9 16.9 %all-to-all-start.1 = ((bf16[64,1,16,2048]{3,2,1,0:T(8,128)(2,1)}), bf16[64,1,16,2048]{3,2,1,0:T(8,128)(2,1)}, u32[]{:S(2)}, u32[]{:S(2)}) async-start(bf16[64,1,16,2048]{3,2,1,0:T(8,128)(2,1)} %bitcast.126), calls=%async_computation.1 | async-start | bytes 8388608 | tf_op jit(solution)/shard_map/all_to_all | solution.py:55
  75.0 95.7 %all-to-all-done.1 = bf16[64,1,16,2048]{3,2,1,0:T(8,128)(2,1)} async-done(((bf16[64,1,16,2048]{3,2,1,0:T(8,128)(2,1)}), bf16[64,1,16,2048]{3,2,1,0:T(8,128)(2,1)}, u32[]{:S(2)}, u32[]{:S(2)}) %all-to-all-start.1) | async-done | bytes 4194336 | tf_op jit(solution)/shard_map/all_to_all | solution.py:55
  170.6 4.5 %fusion.49 = (f32[1024]{0:T(1024)S(1)}, bf16[1,96,1024]{2,1,0:T(8,128)(2,1)}, bf16[1,96,1024]{2,1,0:T(8,128)(2,1)}) fusion(bf16[1,96,1024]{2,1,0:T(8,128)(2,1)S(1)} %copy-done.6, bf16[1,96,1024]{2,1,0:T(8,128)(2,1)S(1)} %copy-done.7, f32[1024]{0:T(1024)S(1)} %reshape.284, bf16[1024,2048]{1,0:T(8,128)(2,1)} %bitcast.5, bf16[1,96,2048]{2,1,0:T(8,128)(2,1)S(1)} %copy-done), kind=kOutput, calls=%fused_computation.45 | convolution fusion | flops 404716544 | bytes 5382144 | tf_op jit(solution)/shard_map/efd,esd->efs/dot_general | solution.py:71
  175.2 0.7 all-gather.4.cloned.1.call-update
  175.9 0.2 all-gather.8.cloned.1.call-start
  176.2 0.5 all-gather.8.cloned.1.call-update
  176.7 0.8 copy.37
  177.4 0.5 broadcast.100
  177.9 11.5 %reduce.14 = bf16[2048,96]{1,0:T(8,128)(2,1)S(1)} reduce(bf16[2048,1,96]{2,1,0:T(2,128)(2,1)S(1)} %bitcast.128, bf16[]{:T(256)} %broadcast.100), dimensions={1}, to_apply=%bitcast.114.reduce_sub_computation | reduce | bytes 786434
  189.5 1.6 reshape.339
  191.1 3.7 %all-to-all-start.3 = ((bf16[8,2,12288]{2,1,0:T(2,128)(2,1)}), bf16[8,2,12288]{2,1,0:T(2,128)(2,1)S(1)}, u32[]{:S(2)}, u32[]{:S(2)}) async-start(bf16[8,2,12288]{2,1,0:T(2,128)(2,1)} %reshape.339), calls=%async_computation.3 | async-start | bytes 786432 | tf_op jit(solution)/shard_map/all_to_all | solution.py:69
  194.8 0.8 copy.34
  195.5 11.5 %reduce.15 = bf16[2048,96]{1,0:T(8,128)(2,1)S(1)} reduce(bf16[2048,1,96]{2,1,0:T(2,128)(2,1)S(1)} %bitcast.129, bf16[]{:T(256)} %broadcast.100), dimensions={1}, to_apply=%bitcast.116.reduce_sub_computation | reduce | bytes 786434
  207.1 1.6 reshape.341
  208.6 4.2 %all-to-all-done.3 = bf16[8,2,12288]{2,1,0:T(2,128)(2,1)S(1)} async-done(((bf16[8,2,12288]{2,1,0:T(2,128)(2,1)}), bf16[8,2,12288]{2,1,0:T(2,128)(2,1)S(1)}, u32[]{:S(2)}, u32[]{:S(2)}) %all-to-all-start.3) | async-done | bytes 393248 | tf_op jit(solution)/shard_map/all_to_all | solution.py:69
  212.9 3.5 all-to-all-start.2
  216.4 0.8 reshape.340
  217.2 0.6 copy.38
  218.0 11.4 %all-to-all-done.2 = bf16[8,2,12288]{2,1,0:T(2,128)(2,1)S(1)} async-done(((bf16[8,2,12288]{2,1,0:T(2,128)(2,1)}), bf16[8,2,12288]{2,1,0:T(2,128)(2,1)S(1)}, u32[]{:S(2)}, u32[]{:S(2)}) %all-to-all-start.2) | async-done | bytes 393248 | tf_op jit(solution)/shard_map/all_to_all | solution.py:68
  229.4 0.8 reshape.342
  230.1 0.6 copy.35
  231.0 21.2 %psum.7 = bf16[1,1024]{1,0:T(2,128)(2,1)S(1)} all-reduce(f32[1,1024]{1,0:T(1,128)S(1)} %bitcast.142), channel_id=1, replica_groups=mesh['exp'=64,'et'=8] {'et'}, use_global_device_ids=true, to_apply=%region_7.8 | all-reduce | flops 1024 | bytes 6144 | tf_op jit(solution)/shard_map/psum | solution.py:80
  252.2 0.7 convert_element_type.140
  252.9 15.5 %all-to-all-start.5 = ((bf16[64,1,16]{2,1,0:T(2,128)(2,1)}), bf16[64,1,16]{2,1,0:T(2,128)(2,1)S(1)}, u32[]{:S(2)}, u32[]{:S(2)}) async-start(bf16[64,1,16]{2,1,0:T(2,128)(2,1)} %convert_element_type.140), calls=%async_computation.5 | async-start | bytes 65536 | tf_op jit(solution)/shard_map/all_to_all | solution.py:113
  268.5 2.0 fusion.30
  270.5 2.9 fusion.37
  273.4 4.3 %all-to-all-done.5 = bf16[64,1,16]{2,1,0:T(2,128)(2,1)S(1)} async-done(((bf16[64,1,16]{2,1,0:T(2,128)(2,1)}), bf16[64,1,16]{2,1,0:T(2,128)(2,1)S(1)}, u32[]{:S(2)}, u32[]{:S(2)}) %all-to-all-start.5) | async-done | bytes 2080 | tf_op jit(solution)/shard_map/all_to_all | solution.py:113
  277.6 6.1 %all-to-all-start.4 = ((bf16[64,1,16,256]{3,2,1,0:T(8,128)(2,1)}), bf16[64,1,16,256]{3,2,1,0:T(8,128)(2,1)S(1)}, u32[]{:S(2)}, u32[]{:S(2)}) async-start(bf16[64,1,16,256]{3,2,1,0:T(8,128)(2,1)} %bitcast.16), calls=%async_computation.4 | async-start | bytes 1048576 | tf_op jit(solution)/shard_map/all_to_all | solution.py:110
  283.7 41.8 %all-gather.8.cloned.1.call-done = bf16[1,1024,2048]{2,1,0:T(8,128)(2,1)} async-done(((bf16[1,1024,256]{2,1,0:T(8,128)(2,1)}), bf16[1,1024,2048]{2,1,0:T(8,128)(2,1)}) %all-gather.8.cloned.1.call-update) | async-done | bytes 4194320 | tf_op jit(solution)/shard_map/all_gather | solution.py:101
  325.6 3.9 %fusion.21 = bf16[1,96,2048]{2,1,0:T(8,128)(2,1)} fusion(bf16[1,1024,2048]{2,1,0:T(8,128)(2,1)} %all-gather.8.cloned.1.call-done, bf16[1,96,1024]{2,1,0:T(8,128)(2,1)S(1)} %copy-done.3), kind=kOutput, calls=%fused_computation.17 | convolution fusion | flops 402849792 | bytes 4784128 | tf_op jit(solution)/shard_map/efs,esp->efp/dot_general | solution.py:105
  329.5 1.5 fusion.24
  331.0 4.1 %fusion.18 = bf16[1,96,2048]{2,1,0:T(8,128)(2,1)} fusion(bf16[1,1024,1,1,1,1,2048]{6,1,5,4,3,2,0:T(8,128)(2,1)} %bitcast.32, f32[1024]{0:T(1024)S(1)} %reshape.284, bf16[1,96,1024]{2,1,0:T(8,128)(2,1)S(1)} %copy-done.6, bf16[1,96,1024]{2,1,0:T(8,128)(2,1)S(1)} %copy-done.7), kind=kOutput, calls=%fused_computation.16 | convolution fusion | flops 409927680 | bytes 4984832 | tf_op jit(solution)/shard_map/efs,esd->efd/dot_general | solution.py:87
  335.3 2.3 gather_fusion.1
  337.6 0.7 copy.42
  338.3 1.9 gather_fusion
  340.3 0.8 bitcast_reduce_fusion
  (45 shorter events, 1.4 us)
Async XLA Ops:
  7.2 163.5 %copy-start = (bf16[1,96,2048]{2,1,0:T(8,128)(2,1)S(1)}, bf16[1,96,2048]{2,1,0:T(8,128)(2,1)}, u32[]{:S(2)}) copy-start(bf16[1,96,2048]{2,1,0:T(8,128)(2,1)} %param.17) | copy-start | bytes 1179652
  14.7 43.1 %all-to-all-start = ((bf16[64,1,16]{2,1,0:T(2,128)(2,1)}), bf16[64,1,16]{2,1,0:T(2,128)(2,1)S(1)}, u32[]{:S(2)}, u32[]{:S(2)}) async-start(bf16[64,1,16]{2,1,0:T(2,128)(2,1)} %convert_element_type.139), calls=%async_computation | async-start | bytes 65536 | tf_op jit(solution)/shard_map/all_to_all | solution.py:62
  57.9 112.8 %copy-start.6 = (bf16[1,96,1024]{2,1,0:T(8,128)(2,1)S(1)}, bf16[1,96,1024]{2,1,0:T(8,128)(2,1)}, u32[]{:S(2)}) copy-start(bf16[1,96,1024]{2,1,0:T(8,128)(2,1)} %param.14) | copy-start | bytes 589828
  57.9 112.8 %copy-start.7 = (bf16[1,96,1024]{2,1,0:T(8,128)(2,1)S(1)}, bf16[1,96,1024]{2,1,0:T(8,128)(2,1)}, u32[]{:S(2)}) copy-start(bf16[1,96,1024]{2,1,0:T(8,128)(2,1)} %param.13) | copy-start | bytes 589828
  57.9 112.8 %all-to-all-start.1 = ((bf16[64,1,16,2048]{3,2,1,0:T(8,128)(2,1)}), bf16[64,1,16,2048]{3,2,1,0:T(8,128)(2,1)}, u32[]{:S(2)}, u32[]{:S(2)}) async-start(bf16[64,1,16,2048]{3,2,1,0:T(8,128)(2,1)} %bitcast.126), calls=%async_computation.1 | async-start | bytes 8388608 | tf_op jit(solution)/shard_map/all_to_all | solution.py:55
  74.7 193.7 %all-gather.6.cloned.1.call-start = ((), (), s32[]{:S(2)}) async-start(), calls=%async_computation.7 | async-start | bytes 1769472 | tf_op jit(solution)/shard_map/all_gather | solution.py:92
  170.6 6.0 %copy-start.4 = (bf16[1,96,2048]{2,1,0:T(8,128)(2,1)S(1)}, bf16[1,96,2048]{2,1,0:T(8,128)(2,1)}, u32[]{:S(2)}) copy-start(bf16[1,96,2048]{2,1,0:T(8,128)(2,1)} %param.16) | copy-start | bytes 1179652
  175.1 19.6 %copy-start.5 = (bf16[1,96,2048]{2,1,0:T(8,128)(2,1)S(1)}, bf16[1,96,2048]{2,1,0:T(8,128)(2,1)}, u32[]{:S(2)}) copy-start(bf16[1,96,2048]{2,1,0:T(8,128)(2,1)} %param.15) | copy-start | bytes 1179652
  175.2 95.3 %all-gather.4.cloned.1.call-start = ((), (), s32[]{:S(2)}) async-start(), calls=%async_computation.6 | async-start | bytes 1769472 | tf_op jit(solution)/shard_map/all_gather | solution.py:91
  175.9 149.6 %all-gather.8.cloned.1.call-start = ((), (), s32[]{:S(2)}) async-start(), calls=%async_computation.8 | async-start | bytes 4718592 | tf_op jit(solution)/shard_map/all_gather | solution.py:101
  191.1 21.8 %all-to-all-start.3 = ((bf16[8,2,12288]{2,1,0:T(2,128)(2,1)}), bf16[8,2,12288]{2,1,0:T(2,128)(2,1)S(1)}, u32[]{:S(2)}, u32[]{:S(2)}) async-start(bf16[8,2,12288]{2,1,0:T(2,128)(2,1)} %reshape.339), calls=%async_computation.3 | async-start | bytes 786432 | tf_op jit(solution)/shard_map/all_to_all | solution.py:69
  212.9 16.5 %all-to-all-start.2 = ((bf16[8,2,12288]{2,1,0:T(2,128)(2,1)}), bf16[8,2,12288]{2,1,0:T(2,128)(2,1)S(1)}, u32[]{:S(2)}, u32[]{:S(2)}) async-start(bf16[8,2,12288]{2,1,0:T(2,128)(2,1)} %reshape.341), calls=%async_computation.2 | async-start | bytes 786432 | tf_op jit(solution)/shard_map/all_to_all | solution.py:68
  231.0 94.6 %copy-start.3 = (bf16[1,96,1024]{2,1,0:T(8,128)(2,1)S(1)}, bf16[1,96,1024]{2,1,0:T(8,128)(2,1)}, u32[]{:S(2)}) copy-start(bf16[1,96,1024]{2,1,0:T(8,128)(2,1)} %get-tuple-element.22) | copy-start | bytes 589828
  252.9 24.7 %all-to-all-start.5 = ((bf16[64,1,16]{2,1,0:T(2,128)(2,1)}), bf16[64,1,16]{2,1,0:T(2,128)(2,1)S(1)}, u32[]{:S(2)}, u32[]{:S(2)}) async-start(bf16[64,1,16]{2,1,0:T(2,128)(2,1)} %convert_element_type.140), calls=%async_computation.5 | async-start | bytes 65536 | tf_op jit(solution)/shard_map/all_to_all | solution.py:113
  270.5 59.0 %copy-start.2 = (bf16[1,96,1024]{2,1,0:T(8,128)(2,1)S(1)}, bf16[1,96,1024]{2,1,0:T(8,128)(2,1)}, u32[]{:S(2)}) copy-start(bf16[1,96,1024]{2,1,0:T(8,128)(2,1)} %get-tuple-element.21) | copy-start | bytes 589828
  277.6 60.7 %all-to-all-start.4 = ((bf16[64,1,16,256]{3,2,1,0:T(8,128)(2,1)}), bf16[64,1,16,256]{3,2,1,0:T(8,128)(2,1)S(1)}, u32[]{:S(2)}, u32[]{:S(2)}) async-start(bf16[64,1,16,256]{3,2,1,0:T(8,128)(2,1)} %bitcast.16), calls=%async_computation.4 | async-start | bytes 1048576 | tf_op jit(solution)/shard_map/all_to_all | solution.py:110
  325.6 3.9 %copy-start.1 = (bf16[1,1024,2048]{2,1,0:T(8,128)(2,1)S(1)}, bf16[1,1024,2048]{2,1,0:T(8,128)(2,1)}, u32[]{:S(2)}) copy-start(bf16[1,1024,2048]{2,1,0:T(8,128)(2,1)} %all-gather.8.cloned.1.call-done) | copy-start | bytes 12582916
Sparse Core Ops, SparseCore 0:
  175.3 38.0 all-gather.5
  216.0 42.1 all-gather.3
  260.3 65.2 all-gather.7
where the time goes:
time: 351 us; the launch traced here: 348 us
  waiting for transfers between devices  159 us (45%)
  starting transfers between devices  57.5 us (16%)
  blocking collectives  46.5 us (13%)
  other arithmetic  26.1 us (7%)
  local copies, waits for them, and re-layouts  25.9 us (7%)
  matrix products  18.9 us (5%)
  between operations  14.1 us (4%)
    all_to_all x1, waiting for transfers between devices, body(): lax.all_to_all(buffer.reshape(exp_count, local_experts, most_rows, whole_...  95.7 us
    all_gather x1, waiting for transfers between devices, body(): piece_rows = lax.all_gather(routed_rows, 'et', axis=2, tiled=True)  41.8 us
    all_gather x1, blocking collectives, body(): whole_grad = lax.all_gather(out_grad, 'et', axis=1, tiled=True)  25.3 us
    unnamed x2, other arithmetic  23.1 us
    psum x1, blocking collectives, body(): score_total = lax.psum(score_local, 'et')  21.2 us
    all_to_all x1, starting transfers between devices, body(): lax.all_to_all(buffer.reshape(exp_count, local_experts, most_rows, whole_...  16.9 us
    all_to_all x1, starting transfers between devices, body(): lax.all_to_all(from_slots(score_total, exp_count).astype(jnp.bfloat16), '...  15.5 us
    all_to_all x1, starting transfers between devices, body(): lax.all_to_all(score_send.astype(jnp.bfloat16), 'exp', split_axis=0, conc...  11.6 us
  transfers between devices with their start and end apart: 9, of which 5 were waited for; matrix products, arithmetic and copies ran while one was open for 16% of the time, Pallas kernels for 0%

commit v1 on v0

v1 whole, which is shorter than its diff:
```python
import functools

import jax
import jax.numpy as jnp
from jax import lax
from jax.experimental import pallas as pl
from jax.experimental.pallas import tpu as pltpu
from jax.sharding import PartitionSpec as P

MESH = pl.DeviceIdType.MESH
BF = jnp.bfloat16
F32 = jnp.float32
NX, NY, NC, NZ, NE = 4, 8, 2, 8, 64
TOK, TOP, W, D, FZ, FF = 64, 8, 256, 2048, 96, 768
META = 512
NR = 528
RA = (0, 320)
RAH = ((0, 160), (160, 160))
RB = (320, 208)
RBH = ((320, 96), (416, 112))
DIRS = (0, 1)


def dot(a, b, dims=((1,), (0,)), precision=None):
    return lax.dot_general(
        a, b, (dims, ((), ())), preferred_element_type=F32, precision=precision
    )


def remote(src, dst, send, recv, target):
    return pltpu.make_async_remote_copy(
        src_ref=src, dst_ref=dst, send_sem=send, recv_sem=recv,
        device_id=target, device_id_type=MESH,
    )


def kernel(
    x_ref, meta_ref, ids_ref, rr_ref, gp_ref, up_ref, gw_ref, uw_ref, dw_ref,
    tg_ref, sg_ref, gg_ref, ug_ref, dg_ref,
    tok, wc, rrp, gup, row_grad, hsp, gfull, sp, stot, acc, wsend, wrecv, rsend, back, sback,
    lsem, zs, zr, ws, wr, ays, ayr, axs, axr, bxs, bxr, bys, byr, prs, prr,
    czs, czr, sps, spr, gs, gr, rs, rr_sem, ss, sr,
):
    e = lax.axis_index("exp")
    z = lax.axis_index("et")
    x = e // 16
    y = lax.rem(e // 2, NY)
    c = lax.rem(e, 2)

    def zz(d):
        return lax.rem(z + d + 16, NZ)

    def yy(d):
        return lax.rem(y + d + 16, NY)

    def xx(d):
        return lax.rem(x + d + 8, NX)

    def at_xy(dx, dy, core):
        return {"exp": (xx(dx) * NY + yy(dy)) * 2 + core}

    barrier = pltpu.get_barrier_semaphore()
    for d in range(1, NZ):
        pl.semaphore_signal(barrier, inc=1, device_id={"et": zz(d)}, device_id_type=MESH)

    def greet(d, carry):
        pl.semaphore_signal(
            barrier, inc=1, device_id={"exp": lax.rem(e + d, NE)}, device_id_type=MESH
        )
        return carry

    lax.fori_loop(1, NE, greet, 0)

    local = [
        pltpu.make_async_copy(x_ref, tok.at[y, x, c, pl.ds(z * TOK, TOK)], lsem.at[0]),
        pltpu.make_async_copy(meta_ref, tok.at[y, x, c, pl.ds(META, 16)], lsem.at[1]),
        pltpu.make_async_copy(gw_ref.at[:, pl.ds(z * W, W)], wc.at[0, z], lsem.at[2]),
        pltpu.make_async_copy(uw_ref.at[:, pl.ds(z * W, W)], wc.at[1, z], lsem.at[3]),
    ]
    for b in range(NY):
        local.append(pltpu.make_async_copy(rr_ref.at[:, b], rrp.at[b], lsem.at[4 + b]))
    for k in local:
        k.start()
    pl.semaphore_wait(barrier, NZ - 1 + NE - 1)

    pend = []

    def go(k):
        k.start()
        pend.append(k)

    ztok = []
    for d in (1, 7, 2, 6, 3, 5, 4):
        k = remote(
            x_ref, tok.at[y, x, c, pl.ds(z * TOK, TOK)], zs.at[d], zr.at[d], {"et": zz(d)}
        )
        go(k)
        ztok.append(k)
    wcols = []
    for d in (1, 7, 2, 6, 3, 5, 4):
        t = zz(d)
        for i, ref in enumerate((gw_ref, uw_ref)):
            k = remote(
                ref.at[:, pl.ds(t * W, W)], wc.at[i, z], ws.at[i, d], wr.at[i, d], {"et": t}
            )
            go(k)
            wcols.append(k)
    for k in local:
        k.wait()

    def permute(b, carry):
        q = lax.broadcasted_iota(jnp.int32, (1024, 128), 0)
        p = lax.broadcasted_iota(jnp.int32, (1024, 128), 1)
        sel = (q == (p // 32) * 256 + b * 32 + lax.rem(p, 32)).astype(F32).astype(BF)
        gup[b, 0:FZ] = dot(gp_ref[...], sel).astype(BF)
        gup[b, FZ : 2 * FZ] = dot(up_ref[...], sel).astype(BF)
        return carry

    lax.fori_loop(0, NY, permute, 0)
    for k in ztok:
        k.wait_recv()

    def sgn(direction):
        return -1 if direction == 0 else 1

    def to_y(direction):
        return at_xy(0, -sgn(direction), c)

    def to_x(direction):
        return at_xy(-sgn(direction), 0, c)

    def a_y(d, s):
        r = RAH[d] if s == 4 else RA
        sl = tok.at[yy(sgn(d) * (s - 1)), x, c, pl.ds(*r)]
        return remote(sl, sl, ays.at[d, s], ayr.at[d, s], to_y(d))

    def a_x(d, g, s):
        r = RAH[d] if s == 2 else RA
        sl = tok.at[yy(g), xx(sgn(d) * (s - 1)), c, pl.ds(*r)]
        return remote(sl, sl, axs.at[d, g % 8, s], axr.at[d, g % 8, s], to_x(d))

    def b_x(d, s):
        r = RBH[d] if s == 2 else RB
        sl = tok.at[y, xx(sgn(d) * (s - 1)), c, pl.ds(*r)]
        return remote(sl, sl, bxs.at[d, s], bxr.at[d, s], to_x(d))

    def b_y(d, q, s):
        r = RBH[d] if s == 4 else RB
        sl = tok.at[yy(sgn(d) * (s - 1)), xx(q), c, pl.ds(*r)]
        return remote(sl, sl, bys.at[d, q % 4, s], byr.at[d, q % 4, s], to_y(d))

    def pair(g):
        sl = tok.at[yy(g), :, c]
        return remote(sl, sl, prs.at[g % 8], prr.at[g % 8], at_xy(0, 0, 1 - c))

    def c_z(d, g, s):
        sl = gfull.at[yy(g), zz(sgn(d) * (s - 1))]
        if s == 4:
            sl = sl.at[pl.ds(d * FZ, FZ)]
        return remote(
            sl, sl, czs.at[d, g % 8, s], czr.at[d, g % 8, s], {"et": zz(-sgn(d))}
        )

    def compute(g):
        pair(g).wait_recv()
        b = yy(g)
        lane = lax.broadcasted_iota(jnp.int32, (1, W), 1)
        ui = lax.broadcasted_iota(jnp.int32, (W, W), 0)
        uj = lax.broadcasted_iota(jnp.int32, (W, W), 1)
        upper = ((ui < uj) & (ui // TOK == uj // TOK)).astype(F32).astype(BF)
        srow = jnp.zeros((8, 128), F32)
        picks = []
        for h in range(2):
            mt = tok[b, 2 * h : 2 * h + 2, :, META : META + 16, :].reshape(4, 16, W).astype(F32)
            hit = (mt[:, 0:8, :] == (e + 1).astype(F32)).astype(F32)
            m = jnp.sum(hit, axis=(0, 1))[None]
            sv = jnp.sum(hit * mt[:, 8:16, :], axis=(0, 1))[None]
            rank = dot(jnp.broadcast_to(m, (8, W)).astype(BF), upper)[0:1]
            want = jnp.where(m > 0, rank.astype(jnp.int32) + 16 * (lane // TOK) + 64 * h, -1)
            slot = lax.broadcasted_iota(jnp.int32, (128, W), 0)
            pick = (slot == want).astype(F32).astype(BF)
            picks.append(pick)
            srow += dot(jnp.broadcast_to(sv, (8, W)).astype(BF), pick, ((1,), (1,)))
        srow = srow[0:1]
        hr = jnp.zeros((FZ, 128), F32)
        for f in range(NZ):
            rows = jnp.zeros((128, W), F32)
            for h in range(2):
                part = tok[b, 2 * h : 2 * h + 2, :, f * TOK : (f + 1) * TOK, :].reshape(W, W)
                rows += dot(picks[h], part)
            rows = rows.astype(BF)
            row_grad[b, :, f * W : (f + 1) * W] = rows
            hr += dot(dw_ref[:, f * W : (f + 1) * W], rows, ((1,), (1,)))
        gate = gup[b, 0:FZ].astype(F32)
        up = gup[b, FZ : 2 * FZ].astype(F32)
        sig = jax.nn.sigmoid(gate)
        silu = gate * sig
        hidden = (silu * up).astype(BF).astype(F32)
        sp[z, pl.ds(b, 1), :] = jnp.sum(hidden * hr, axis=0, keepdims=True)
        hg = srow * hr
        gfull[b, z, 0:FZ] = (hg * up * sig * (1.0 + gate * (1.0 - sig))).astype(BF)
        gfull[b, z, FZ : 2 * FZ] = (hg * silu).astype(BF)
        hsp[b] = (hidden * srow).astype(BF)
        for d in DIRS:
            go(c_z(d, g, 1))

    def advance(g, s):
        for d in DIRS:
            c_z(d, g, s).wait_recv()
            if s < 4:
                go(c_z(d, g, s + 1))

    def weights_part(g, first):
        b = yy(g)
        for i in range(2):
            part = dot(gfull[b, :, i * FZ : (i + 1) * FZ, :].reshape(FF, 128), rrp[b].reshape(128, W))
            if first:
                acc[i] = part
            else:
                acc[i] += part

    def rows_part(g):
        b = yy(g)
        out = dot(gfull[b, :, 0:FZ, :].reshape(FF, 128), wc[0].reshape(FF, W), ((0,), (0,)))
        out += dot(
            gfull[b, :, FZ : 2 * FZ, :].reshape(FF, 128), wc[1].reshape(FF, W), ((0,), (0,))
        )
        rsend[b] = out.astype(BF).reshape(NX, NC, 16, W)

    for d in DIRS:
        go(b_x(d, 1))
    for d in DIRS:
        go(a_y(d, 1))
    for d in DIRS:
        go(a_x(d, 0, 1))
    for d in DIRS:
        go(b_y(d, 0, 1))
    for d in DIRS:
        b_x(d, 1).wait_recv()
        go(b_x(d, 2))
    for q in (-1, 1):
        for d in DIRS:
            go(b_y(d, q, 1))
    for d in DIRS:
        b_x(d, 2).wait_recv()
    for d in DIRS:
        go(b_y(d, 2, 1))

    def groups(k):
        return [0] if k == 0 else ([4] if k == 4 else [k, -k])

    order = []
    for k in range(5):
        order += groups(k)

    def step_bx(q, k):
        for d in DIRS:
            b_y(d, q, k).wait_recv()
            if k < 4:
                go(b_y(d, q, k + 1))

    def step_ax(g):
        for d in DIRS:
            a_x(d, g, 1).wait_recv()
            go(a_x(d, g, 2))

    def finish(g):
        for d in DIRS:
            a_x(d, g, 2).wait_recv()
        go(pair(g))

    for k in range(1, 5):
        for d in DIRS:
            a_y(d, k).wait_recv()
            if k < 4:
                go(a_y(d, k + 1))
                for dd in DIRS:
                    go(a_x(dd, sgn(d) * k, 1))
        if k == 4:
            for dd in DIRS:
                go(a_x(dd, 4, 1))
        prev = groups(k - 1)
        step_bx(0, k)
        step_ax(prev[0])
        step_bx(1, k)
        if len(prev) > 1:
            step_ax(prev[1])
        step_bx(-1, k)
        step_bx(2, k)
        for g in prev:
            finish(g)
    step_ax(4)
    finish(4)

    for g in order:
        compute(g)
    for d in range(1, NZ):
        go(remote(sp.at[z], sp.at[z], sps.at[d], spr.at[d], {"et": zz(d)}))
    for s in range(1, 5):
        for g in order:
            advance(g, s)
    for d in range(1, NZ):
        remote(sp.at[z], sp.at[z], sps.at[d], spr.at[d], {"et": zz(d)}).wait_recv()
    for i, g in enumerate(order):
        weights_part(g, i == 0)

    for i in range(2):
        wsend[i] = acc[i].astype(BF).reshape(NZ, FZ, W)
    wout = []
    for d in (4, 3, 5, 2, 6, 1, 7):
        t = zz(d)
        for i in range(2):
            k = remote(wsend.at[i, t], wrecv.at[i, z], gs.at[i, d], gr.at[i, d], {"et": t})
            go(k)
            wout.append(k)

    total = sp[0]
    for i in range(1, NZ):
        total = total + sp[i]
    stot[...] = total.reshape(NY, 1, 128)
    for k in wcols:
        k.wait_recv()
    for g in order:
        rows_part(g)

    def score_to(d):
        t = lax.rem(e + d, NE)
        ty = lax.rem(t // 2, NY)
        return remote(stot.at[ty], sback.at[e], ss.at[d], sr.at[d], {"exp": t})

    def rows_to(d):
        t = lax.rem(e + d, NE)
        src = rsend.at[lax.rem(t // 2, NY), t // 16, lax.rem(t, 2)]
        return remote(src, back.at[e], rs.at[d], rr_sem.at[d], {"exp": t})

    def send_back(d, carry):
        rows_to(d).start()
        score_to(d).start()
        return carry

    lax.fori_loop(1, NE, send_back, 0)
    keep = [
        pltpu.make_async_copy(rsend.at[y, x, c], back.at[e], lsem.at[0]),
        pltpu.make_async_copy(stot.at[y], sback.at[e], lsem.at[1]),
    ]
    for k in keep:
        k.start()

    hs = jnp.concatenate([hsp[b] for b in range(NY)], axis=1)
    for f in range(NZ):
        rows = row_grad[:, :, f * W : (f + 1) * W].reshape(1024, W)
        dg_ref[:, f * W : (f + 1) * W] = dot(hs, rows).astype(BF)

    ids = ids_ref[...]
    lane_e = lax.broadcasted_iota(jnp.int32, (TOK, NE), 1)
    names = jnp.zeros((TOK, NE), F32)
    for k in range(TOP):
        names += (ids[:, k : k + 1] == lane_e).astype(F32)
    ti = lax.broadcasted_iota(jnp.int32, (TOK, TOK), 0)
    tj = lax.broadcasted_iota(jnp.int32, (TOK, TOK), 1)
    rank = dot((tj < ti).astype(F32).astype(BF), names.astype(BF))
    rank = jnp.where(names > 0, rank, -1.0)
    ei = lax.broadcasted_iota(jnp.int32, (NE, 1024), 0)
    ej = lax.broadcasted_iota(jnp.int32, (NE, 1024), 1)
    spread = (ej // 16 == ei).astype(F32).astype(BF)
    place = lax.rem(lax.broadcasted_iota(jnp.int32, (TOK, 1024), 1), 16).astype(F32)
    gather = (dot(rank.astype(BF), spread) == place).astype(F32).astype(BF)

    for k in keep:
        k.wait()

    def wait_back(d, carry):
        rows_to(d).wait_recv()
        score_to(d).wait_recv()
        return carry

    lax.fori_loop(1, NE, wait_back, 0)
    tg_ref[...] = dot(gather, back[...].reshape(1024, W)).astype(BF)
    li = lax.broadcasted_iota(jnp.int32, (16, 128), 0)
    lj = lax.broadcasted_iota(jnp.int32, (16, 128), 1)
    mine = (lj == x * 32 + c * 16 + li).astype(F32)
    slots = dot(mine, sback[...].reshape(NE, 128), ((1,), (1,)), lax.Precision.HIGHEST)
    value = jnp.zeros((TOK, NE), F32)
    for j in range(16):
        value += jnp.where(rank == j, slots[j : j + 1, :], 0.0)
    lane_k = lax.broadcasted_iota(jnp.int32, (TOK, TOP), 1)
    score = jnp.zeros((TOK, TOP), F32)
    for k in range(TOP):
        one = jnp.sum(jnp.where(ids[:, k : k + 1] == lane_e, value, 0.0), axis=1, keepdims=True)
        score = jnp.where(lane_k == k, one, score)
    sg_ref[...] = score

    for i in range(2):
        wrecv[i, z] = wsend[i, z]
    for k in wout:
        k.wait_recv()
    for i, ref in enumerate((gg_ref, ug_ref)):
        for t in range(NZ):
            ref[:, t * W : (t + 1) * W] = wrecv[i, t]

    for k in pend:
        k.wait_send()

    def wait_sent(d, carry):
        rows_to(d).wait_send()
        score_to(d).wait_send()
        return carry

    lax.fori_loop(1, NE, wait_sent, 0)


def body(
    out_grad, gate_scores, expert_ids, routed_rows, gate_pre, up_pre,
    gate_weight, up_weight, down_weight,
):
    e = lax.axis_index("exp")
    lane = lax.rem(e // 16, 2) * 2 + lax.rem(e, 2)
    pair = jnp.concatenate(
        [(expert_ids + 1).astype(F32).T, gate_scores.T], axis=0
    ).astype(BF)
    meta = jnp.where(
        (jnp.arange(W, dtype=jnp.int32) // TOK == lane)[None, :], jnp.tile(pair, (1, 4)), 0
    ).astype(BF)
    vmem = pl.BlockSpec(memory_space=pltpu.VMEM)
    hbm = pl.BlockSpec(memory_space=pl.ANY)
    dma = pltpu.SemaphoreType.DMA
    outs = pl.pallas_call(
        kernel,
        out_shape=(
            jax.ShapeDtypeStruct((TOK, W), BF),
            jax.ShapeDtypeStruct((TOK, TOP), F32),
            jax.ShapeDtypeStruct((FZ, D), BF),
            jax.ShapeDtypeStruct((FZ, D), BF),
            jax.ShapeDtypeStruct((FZ, D), BF),
        ),
        in_specs=[vmem, vmem, vmem, hbm, vmem, vmem, vmem, vmem, vmem],
        out_specs=(vmem,) * 5,
        scratch_shapes=[
            pltpu.VMEM((NY, NX, NC, NR, W), BF),
            pltpu.VMEM((2, NZ, FZ, W), BF),
            pltpu.VMEM((NY, NX, 32, W), BF),
            pltpu.VMEM((NY, 2 * FZ, 128), BF),
            pltpu.VMEM((NY, 128, D), BF),
            pltpu.VMEM((NY, FZ, 128), BF),
            pltpu.VMEM((NY, NZ, 2 * FZ, 128), BF),
            pltpu.VMEM((NZ, NY, 128), F32),
            pltpu.VMEM((NY, 1, 128), F32),
            pltpu.VMEM((2, FF, W), F32),
            pltpu.VMEM((2, NZ, FZ, W), BF),
            pltpu.VMEM((2, NZ, FZ, W), BF),
            pltpu.VMEM((NY, NX, NC, 16, W), BF),
            pltpu.VMEM((NE, 16, W), BF),
            pltpu.VMEM((NE, 1, 128), F32),
            dma((12,)),
            dma((8,)), dma((8,)),
            dma((2, 8)), dma((2, 8)),
            dma((2, 5)), dma((2, 5)),
            dma((2, 8, 3)), dma((2, 8, 3)),
            dma((2, 3)), dma((2, 3)),
            dma((2, 4, 5)), dma((2, 4, 5)),
            dma((8,)), dma((8,)),
            dma((2, 8, 5)), dma((2, 8, 5)),
            dma((8,)), dma((8,)),
            dma((2, 8)), dma((2, 8)),
            dma((NE,)), dma((NE,)),
            dma((NE,)), dma((NE,)),
        ],
        compiler_params=pltpu.CompilerParams(
            collective_id=0, has_side_effects=True, vmem_limit_bytes=56 << 20
        ),
        name="expert_backward",
    )(
        out_grad, meta, expert_ids, routed_rows.reshape(NX, NY, 32, W),
        gate_pre.reshape(FZ, 1024), up_pre.reshape(FZ, 1024),
        gate_weight.reshape(FZ, D), up_weight.reshape(FZ, D), down_weight.reshape(FZ, D),
    )
    token_grad, score_grad, gate_out, up_out, down_out = outs
    return token_grad, score_grad, gate_out[None], up_out[None], down_out[None]


def solution(mesh):
    return jax.shard_map(
        body,
        mesh=mesh,
        in_specs=(
            P("exp", "et"), P("exp", None), P("exp", None), P("exp", None, "et"),
            P("exp", "et", None), P("exp", "et", None), P("exp", "et", None),
            P("exp", "et", None), P("exp", "et", None),
        ),
        out_specs=(
            P("exp", "et"), P("exp", None), P("exp", "et", None), P("exp", "et", None),
            P("exp", "et", None),
        ),
        check_vma=False,
    )
```

time: 351 us -> 149 us (0.42)
  waiting for transfers between devices: 159 us -> 0 us
  Pallas kernels: 0 us -> 140 us
  starting transfers between devices: 57.5 us -> 0 us
  blocking collectives: 46.5 us -> 0 us
  other arithmetic: 26.1 us -> 0.63 us
  matrix products: 18.9 us -> 0 us
  local copies, waits for them, and re-layouts: 25.9 us -> 7.23 us
  between operations: 14.1 us -> 0.7 us
    pallas_call x0 -> x1, Pallas kernels: none -> 140 us  [body(): pl.pallas_call(kernel, out_shape=(jax.ShapeDtypeStruct((TOK, W), BF), jax...]
    all_to_all x6 -> x0, waiting for transfers between devices: 116 us -> none  [the longest x1 95.7 us: body(): lax.all_to_all(buffer.reshape(exp_count, local_experts, most_rows, whole_...]
    all_to_all x6 -> x0, starting transfers between devices: 57.2 us -> none  [the longest x1 16.9 us: body(): lax.all_to_all(buffer.reshape(exp_count, local_experts, most_rows, whole_...]
    all_gather x3 -> x0, waiting for transfers between devices: 41.9 us -> none  [the longest x1 41.8 us: body(): piece_rows = lax.all_gather(routed_rows, 'et', axis=2, tiled=True)]
    all_gather x1 -> x0, blocking collectives: 25.3 us -> none  [body(): whole_grad = lax.all_gather(out_grad, 'et', axis=1, tiled=True)]
    unnamed x2 -> x0, other arithmetic: 23.1 us -> none
    psum x1 -> x0, blocking collectives: 21.2 us -> none  [body(): score_total = lax.psum(score_local, 'et')]
    dot_general x6 -> x0, matrix products: 18.9 us -> none  [the longest x1 4.51 us: body(): jnp.einsum('efd,esd->efs', down_weight, row_grad, preferred_element_type=...]
  transfers between devices with their start and end apart: 9 -> 0, of which waited for: 5 -> 0; matrix products, arithmetic and copies ran while one was open for 16% -> 0% of each run, Pallas kernels for 0% -> 0%
where the time goes in v1:
time: 149 us
  Pallas kernels  140 us (94%)
  local copies, waits for them, and re-layouts  7.23 us (5%)
    pallas_call x1, Pallas kernels, body(): pl.pallas_call(kernel, out_shape=(jax.ShapeDtypeStruct((TOK, W), BF), jax...  140 us
    unnamed x16, local copies, waits for them, and re-layouts  7.13 us

profile of v1, /device:TPU:1, one launch (start us, length us, event | category | flops | bytes accessed | tf_op | source)
XLA Modules:
  0.0 148.8 jit_solution(9176069491593044659)
XLA Ops:
  0.7 0.0 copy-start.4
  0.7 0.0 copy-start.3
  0.7 0.7 copy-done.4
  1.4 0.0 copy-done.3
  1.4 0.1 tile.10
  1.5 0.6 broadcast_select_fusion.meta_ref
  2.1 0.7 copy.14.ids_ref
  2.8 140.3 %expert_backward.1 = (bf16[64,256]{1,0:T(8,128)(2,1)}, f32[64,8]{1,0:T(8,128)}, bf16[96,2048]{1,0:T(8,128)(2,1)}, bf16[96,2048]{1,0:T(8,128)(2,1)}, bf16[96,2048]{1,0:T(8,128)(2,1)}) custom-call(bf16[64,256]{1,0:T(8,128)(2,1)} %x_ref.1, bf16[16,256]{1,0:T(8,128)(2,1)} %broadcast_select_fusion.meta_ref, s32[64,8]{1,0:T(8,128)} %copy.14.ids_ref, ...), custom_call_target="tpu_custom_call" | custom-call | tf_op jit(solution)/shard_map/expert_backward/pallas_call | solution.py:427
  143.1 0.0 copy-start.2
  143.1 1.4 copy.15
  144.5 0.0 copy-done.2
  144.5 0.6 copy.20
  145.1 0.0 copy-start.1
  145.1 1.8 %copy.21 = bf16[1,96,2048]{2,1,0:T(8,128)(2,1)} copy(bf16[1,96,2048]{2,1,0:T(8,128)(2,1)} %bitcast.16) | data formatting | bytes 786432
  146.9 0.0 copy-done.1
  146.9 0.0 copy-start
  146.9 0.7 copy.22
  147.7 0.4 copy-done
  148.1 0.7 copy.23
  (5 shorter events, 0.0 us)
Async XLA Ops:
  0.7 0.7 copy-start.4
  0.7 0.7 copy-start.3
  143.1 1.4 copy-start.2
  145.1 1.8 %copy-start.1 = (bf16[96,2048]{1,0:T(8,128)(2,1)S(1)}, bf16[96,2048]{1,0:T(8,128)(2,1)}, u32[]{:S(2)}) copy-start(bf16[96,2048]{1,0:T(8,128)(2,1)} %get-tuple-element.13) | copy-start | bytes 1179652
  146.9 1.1 copy-start

commit v2 on v1

v2 whole, which is shorter than its diff:
```python
import functools

import jax
import jax.numpy as jnp
from jax import lax
from jax.experimental import pallas as pl
from jax.experimental.pallas import tpu as pltpu
from jax.sharding import PartitionSpec as P

MESH = pl.DeviceIdType.MESH
BF = jnp.bfloat16
F32 = jnp.float32
NX, NY, NC, NZ, NE = 4, 8, 2, 8, 64
TOK, TOP, W, D, FZ, FF = 64, 8, 256, 2048, 96, 768
META = 512
NR = 528
RA = (0, 320)
RAH = ((0, 160), (160, 160))
RB = (320, 208)
RBH = ((320, 96), (416, 112))
DIRS = (0, 1)
STEPPED = (0, 1, -1, 2, -2, 3, -3, 4)


def dot(a, b, dims=((1,), (0,)), precision=None):
    return lax.dot_general(
        a, b, (dims, ((), ())), preferred_element_type=F32, precision=precision
    )


def remote(src, dst, send, recv, target):
    return pltpu.make_async_remote_copy(
        src_ref=src, dst_ref=dst, send_sem=send, recv_sem=recv,
        device_id=target, device_id_type=MESH,
    )


def kernel(
    x_ref, ids_ref, score_ref, rr_ref, gp_hbm, up_hbm, gw_ref, uw_ref, dw_hbm,
    tg_ref, sg_ref, gg_ref, ug_ref, dg_ref,
    tok, wc, rrp, gp_ref, up_ref, dw_ref, gup, row_grad, hsp, gfull, sp, stot, acc, wsend, rsend, back, sback,
    lsem, zs, zr, ws, wr, fhs, fhr, ays, ayr, axs, axr, bxs, bxr, bys, byr, prs, prr,
    czs, czr, sps, spr, gs, gr, rs, rr_sem, ss, sr,
):
    e = lax.axis_index("exp")
    z = lax.axis_index("et")
    x = e // 16
    y = lax.rem(e // 2, NY)
    c = lax.rem(e, 2)

    def zz(d):
        return lax.rem(z + d + 16, NZ)

    def yy(d):
        return lax.rem(y + d + 16, NY)

    def xx(d):
        return lax.rem(x + d + 8, NX)

    def at_xy(dx, dy, core):
        return {"exp": (xx(dx) * NY + yy(dy)) * 2 + core}

    barrier = pltpu.get_barrier_semaphore()
    for d in range(1, NZ):
        pl.semaphore_signal(barrier, inc=1, device_id={"et": zz(d)}, device_id_type=MESH)

    near = (at_xy(1, 0, c), at_xy(-1, 0, c), at_xy(0, 1, c), at_xy(0, -1, c), at_xy(0, 0, 1 - c))
    for t in near:
        pl.semaphore_signal(barrier, inc=1, device_id=t, device_id_type=MESH)

    local = [
        pltpu.make_async_copy(x_ref, tok.at[y, x, c, pl.ds(z * TOK, TOK)], lsem.at[0]),
        pltpu.make_async_copy(gp_hbm, gp_ref, lsem.at[1]),
        pltpu.make_async_copy(up_hbm, up_ref, lsem.at[2]),
        pltpu.make_async_copy(dw_hbm, dw_ref, lsem.at[3]),
        pltpu.make_async_copy(gw_ref.at[:, pl.ds(z * W, W)], wc.at[0, z], lsem.at[12]),
        pltpu.make_async_copy(uw_ref.at[:, pl.ds(z * W, W)], wc.at[1, z], lsem.at[13]),
    ]
    for b in range(NY):
        local.append(pltpu.make_async_copy(rr_ref.at[:, b], rrp.at[b], lsem.at[4 + b]))
    for k in local:
        k.start()
    place = lax.rem(x, 2) * 2 + c
    pair_rows = jnp.concatenate(
        [(ids_ref[...] + 1).astype(F32), score_ref[...]], axis=0
    )
    pair_rows = jnp.concatenate([pair_rows] * 4, axis=1)
    lane_block = lax.broadcasted_iota(jnp.int32, (16, W), 1) // TOK
    tok[y, x, c, META : META + 16, :] = jnp.where(lane_block == place, pair_rows, 0.0).astype(BF)
    pl.semaphore_wait(barrier, NZ - 1 + len(near))

    pend = []

    def go(k):
        k.start()
        pend.append(k)

    ztok = {}
    for d in (1, 7, 2, 6, 3, 5, 4):
        k = remote(
            x_ref, tok.at[y, x, c, pl.ds(z * TOK, TOK)], zs.at[d], zr.at[d], {"et": zz(d)}
        )
        go(k)
        ztok[d] = k
    wcols = []

    def send_columns(order):
        for d in order:
            t = zz(d)
            for i, ref in enumerate((gw_ref, uw_ref)):
                k = remote(
                    ref.at[:, pl.ds(t * W, W)], wc.at[i, z], ws.at[i, d], wr.at[i, d], {"et": t}
                )
                go(k)
                wcols.append(k)

    def permute(b, carry):
        q = lax.broadcasted_iota(jnp.int32, (1024, 128), 0)
        p = lax.broadcasted_iota(jnp.int32, (1024, 128), 1)
        sel = (q == (p // 32) * 256 + b * 32 + lax.rem(p, 32)).astype(F32).astype(BF)
        gup[b, 0:FZ] = dot(gp_ref[...], sel).astype(BF)
        gup[b, FZ : 2 * FZ] = dot(up_ref[...], sel).astype(BF)
        return carry

    def sgn(direction):
        return -1 if direction == 0 else 1

    def to_y(direction):
        return at_xy(0, -sgn(direction), c)

    def to_x(direction):
        return at_xy(-sgn(direction), 0, c)

    def a_y(d, s):
        r = RAH[d] if s == 4 else RA
        sl = tok.at[yy(sgn(d) * (s - 1)), x, c, pl.ds(*r)]
        if s == 1:
            return remote(sl, sl, fhs.at[0, d, 0], fhr.at[0, d, 0], to_y(d))
        return remote(sl, sl, ays.at[d, s], ayr.at[d, s], to_y(d))

    def a_x(d, g, s):
        r = RAH[d] if s == 2 else RA
        sl = tok.at[yy(g), xx(sgn(d) * (s - 1)), c, pl.ds(*r)]
        if g == 0 and s == 1:
            return remote(sl, sl, fhs.at[1, d, 0], fhr.at[1, d, 0], to_x(d))
        return remote(sl, sl, axs.at[d, g % 8, s], axr.at[d, g % 8, s], to_x(d))

    def b_x(d, s):
        r = RBH[d] if s == 2 else RB
        sl = tok.at[y, xx(sgn(d) * (s - 1)), c, pl.ds(*r)]
        if s == 1:
            return remote(sl, sl, fhs.at[1, d, 1], fhr.at[1, d, 1], to_x(d))
        return remote(sl, sl, bxs.at[d, s], bxr.at[d, s], to_x(d))

    def b_y(d, q, s):
        r = RBH[d] if s == 4 else RB
        sl = tok.at[yy(sgn(d) * (s - 1)), xx(q), c, pl.ds(*r)]
        if q == 0 and s == 1:
            return remote(sl, sl, fhs.at[0, d, 1], fhr.at[0, d, 1], to_y(d))
        return remote(sl, sl, bys.at[d, q % 4, s], byr.at[d, q % 4, s], to_y(d))

    def pair(g, i):
        sl = tok.at[yy(g), :, c, pl.ds(*(RA, RB)[i])]
        return remote(sl, sl, prs.at[i, g % 8], prr.at[i, g % 8], at_xy(0, 0, 1 - c))

    def c_z(d, g, s):
        relayed = s == 2 and g in STEPPED
        held = 1 if relayed else (0 if s < 3 else 2)
        sl = gfull.at[yy(g), zz(sgn(d) * held)]
        if s == 4:
            sl = sl.at[pl.ds(d * FZ, FZ)]
        far = s - held
        return remote(
            sl, sl, czs.at[d, g % 8, s], czr.at[d, g % 8, s], {"et": zz(-sgn(d) * far)}
        )

    def compute(g):
        for i in range(2):
            pair(g, i).wait_recv()
        b = yy(g)
        lane = lax.broadcasted_iota(jnp.int32, (1, W), 1)
        ui = lax.broadcasted_iota(jnp.int32, (W, W), 0)
        uj = lax.broadcasted_iota(jnp.int32, (W, W), 1)
        upper = ((ui < uj) & (ui // TOK == uj // TOK)).astype(F32).astype(BF)
        srow = jnp.zeros((8, 128), F32)
        picks = []
        for h in range(2):
            mt = tok[b, 2 * h : 2 * h + 2, :, META : META + 16, :].reshape(4, 16, W).astype(F32)
            hit = (mt[:, 0:8, :] == (e + 1).astype(F32)).astype(F32)
            m = jnp.sum(hit, axis=(0, 1))[None]
            sv = jnp.sum(hit * mt[:, 8:16, :], axis=(0, 1))[None]
            rank = dot(jnp.broadcast_to(m, (8, W)).astype(BF), upper)[0:1]
            want = jnp.where(m > 0, rank.astype(jnp.int32) + 16 * (lane // TOK) + 64 * h, -1)
            slot = lax.broadcasted_iota(jnp.int32, (128, W), 0)
            pick = (slot == want).astype(F32).astype(BF)
            picks.append(pick)
            srow += dot(jnp.broadcast_to(sv, (8, W)).astype(BF), pick, ((1,), (1,)))
        srow = srow[0:1]
        hr = jnp.zeros((FZ, 128), F32)
        for f in range(NZ):
            rows = jnp.zeros((128, W), F32)
            for h in range(2):
                part = tok[b, 2 * h : 2 * h + 2, :, f * TOK : (f + 1) * TOK, :].reshape(W, W)
                rows += dot(picks[h], part)
            rows = rows.astype(BF)
            row_grad[b, :, f * W : (f + 1) * W] = rows
            hr += dot(dw_ref[:, f * W : (f + 1) * W], rows, ((1,), (1,)))
        gate = gup[b, 0:FZ].astype(F32)
        up = gup[b, FZ : 2 * FZ].astype(F32)
        sig = jax.nn.sigmoid(gate)
        silu = gate * sig
        hidden = (silu * up).astype(BF).astype(F32)
        sp[z, pl.ds(b, 1), :] = jnp.sum(hidden * hr, axis=0, keepdims=True)
        hg = srow * hr
        gfull[b, z, 0:FZ] = (hg * up * sig * (1.0 + gate * (1.0 - sig))).astype(BF)
        gfull[b, z, FZ : 2 * FZ] = (hg * silu).astype(BF)
        hsp[b] = (hidden * srow).astype(BF)
        for s in (1,) if g in STEPPED else (2, 1):
            for d in DIRS:
                go(c_z(d, g, s))

    def step(g):
        for d in DIRS:
            c_z(d, g, 1).wait_recv()
            go(c_z(d, g, 2))

    def relay(g):
        for d in DIRS:
            c_z(d, g, 2).wait_recv()
            for s in (3, 4):
                go(c_z(d, g, s))

    def collect(g):
        for s in (3, 4) if g in STEPPED else (1, 3, 4):
            for d in DIRS:
                c_z(d, g, s).wait_recv()

    def weights_part(g, first):
        b = yy(g)
        for i in range(2):
            part = dot(gfull[b, :, i * FZ : (i + 1) * FZ, :].reshape(FF, 128), rrp[b].reshape(128, W))
            if first:
                acc[i] = part
            else:
                acc[i] += part

    def rows_part(g):
        b = yy(g)
        out = dot(gfull[b, :, 0:FZ, :].reshape(FF, 128), wc[0].reshape(FF, W), ((0,), (0,)))
        out += dot(
            gfull[b, :, FZ : 2 * FZ, :].reshape(FF, 128), wc[1].reshape(FF, W), ((0,), (0,))
        )
        rsend[b] = out.astype(BF).reshape(NX, NC, 16, W)

    def piece(d, axis, src, rows, part):
        dst = tok.at[y, x, c, rows]
        return remote(
            dst if src is None else src, dst, fhs.at[axis, d, part], fhr.at[axis, d, part],
            (to_y, to_x)[axis](d),
        )

    def send_piece(src, rows, part):
        for axis in (1, 0):
            for d in DIRS:
                piece(d, axis, src, rows, part).start()

    send_piece(None, pl.ds(META, 16), 1)
    send_piece(x_ref, pl.ds(z * TOK, TOK), z // 5)
    for d in (1, 7, 2, 6, 3, 5, 4):
        ztok[d].wait_recv()
        f = zz(-d)
        send_piece(None, pl.ds(f * TOK, TOK), f // 5)
    for d in DIRS:
        pend.extend([a_y(d, 1), a_x(d, 0, 1), b_x(d, 1), b_y(d, 0, 1)])
    send_columns((1, 7, 2, 6, 3, 5, 4))
    for k in local:
        k.wait()
    lax.fori_loop(0, NY, permute, 0)

    order = (0, 1, -1, 2, -2, 3, -3, 4)
    done = []
    unsent = []

    def ax0(g):
        for d in DIRS:
            go(a_x(d, g, 1))

    def ax1(g):
        for d in DIRS:
            a_x(d, g, 1).wait_recv()
            go(a_x(d, g, 2))

    def ay(k):
        for d in DIRS:
            a_y(d, k).wait_recv()
            if k < 4:
                go(a_y(d, k + 1))

    def bx1():
        for d in DIRS:
            b_x(d, 1).wait_recv()
            go(b_x(d, 2))
        for q in (-1, 1):
            for d in DIRS:
                go(b_y(d, q, 1))

    def bx2():
        for d in DIRS:
            b_x(d, 2).wait_recv()
        for d in DIRS:
            go(b_y(d, 2, 1))

    def by(q, k):
        for d in DIRS:
            b_y(d, q, k).wait_recv()
            if k < 4:
                go(b_y(d, q, k + 1))

    def pb(g):
        go(pair(g, 1))

    def fin(g):
        for d in DIRS:
            a_x(d, g, 2).wait_recv()
        go(pair(g, 0))

    def take(g):
        collect(g)
        weights_part(g, not done)
        if not done:
            for k in wcols:
                k.wait_recv()
        rows_part(g)
        done.append(g)
        unsent.append(g)

    comp = compute
    plan = [
        (bx1,),
        (ay, 1),
        (ax0, 1),
        (ax0, -1),
        (bx2,),
        (pb, 0),
        (ax1, 0),
        (ay, 2),
        (ax0, 2),
        (ax0, -2),
        (by, 0, 1),
        (by, 1, 1),
        (fin, 0),
        (ax1, 1),
        (ay, 3),
        (by, -1, 1),
        (by, 2, 1),
        (pb, 1),
        (pb, -1),
        (comp, 0),
        (ax1, -1),
        (ax0, 3),
        (ax0, -3),
        (by, 0, 2),
        (fin, 1),
        (ay, 4),
        (by, 1, 2),
        (ax1, 2),
        (comp, 1),
        (step, 0),
        (by, -1, 2),
        (ax0, 4),
        (fin, -1),
        (by, 2, 2),
        (pb, 2),
        (pb, -2),
        (comp, -1),
        (relay, 0),
        (step, 1),
        (ax1, -2),
        (by, 0, 3),
        (fin, 2),
        (by, 1, 3),
        (ax1, 3),
        (comp, 2),
        (relay, 1),
        (step, -1),
        (by, -1, 3),
        (fin, -2),
        (by, 2, 3),
        (pb, 3),
        (pb, -3),
        (comp, -2),
        (take, 0),
        (relay, -1),
        (step, 2),
        (ax1, -3),
        (by, 0, 4),
        (fin, 3),
        (ax1, 4),
        (by, 1, 4),
        (comp, 3),
        (take, 1),
        (relay, 2),
        (step, -2),
        (by, -1, 4),
        (by, 2, 4),
        (pb, 4),
        (fin, -3),
        (comp, -3),
        (take, -1),
        (relay, -2),
        (step, 3),
        (fin, 4),
        (comp, 4),
        (take, 2),
        (relay, 3),
        (step, -3),
    ]
    for event, *given in plan:
        event(*given)

    def target_rows(t):
        src = rsend.at[lax.rem(t // 2, NY), t // 16, lax.rem(t, 2)]
        return src

    def rows_to(t):
        return remote(target_rows(t), back.at[e], rs.at[t], rr_sem.at[e], {"exp": t})

    def rows_from(t):
        return remote(target_rows(e), back.at[t], rs.at[t], rr_sem.at[t], {"exp": t})

    def score_to(t):
        return remote(
            stot.at[lax.rem(t // 2, NY)], sback.at[e], ss.at[t], sr.at[e], {"exp": t}
        )

    def score_from(t):
        return remote(stot.at[y], sback.at[t], ss.at[t], sr.at[t], {"exp": t})

    def send_rows(g):
        for dx in (0, 1, -1, 2):
            for core in range(2):
                if g == 0 and dx == 0:
                    if core == 0:
                        rows_to(at_xy(0, 0, 1 - c)["exp"]).start()
                    continue
                rows_to(at_xy(dx, g, core)["exp"]).start()

    for d in range(1, NZ):
        go(remote(sp.at[z], sp.at[z], sps.at[d], spr.at[d], {"et": zz(d)}))
    step(4)
    if unsent:
        send_rows(unsent.pop(0))
    relay(-3)
    if unsent:
        send_rows(unsent.pop(0))
    relay(4)
    if unsent:
        send_rows(unsent.pop(0))
    take(-2)
    send_rows(unsent.pop(0))
    take(3)
    send_rows(unsent.pop(0))
    take(-3)
    send_rows(unsent.pop(0))
    take(4)
    for i in range(2):
        wsend[i] = acc[i].astype(BF).reshape(NZ, FZ, W)
    wout = []
    for d in (4, 3, 5, 2, 6, 1, 7):
        t = zz(d)
        for i, ref in enumerate((gg_ref, ug_ref)):
            k = remote(
                wsend.at[i, t], ref.at[:, pl.ds(z * W, W)], gs.at[i, d], gr.at[i, d], {"et": t}
            )
            go(k)
            wout.append(k)
    for g in unsent:
        send_rows(g)
    for d in range(1, NZ):
        remote(sp.at[z], sp.at[z], sps.at[d], spr.at[d], {"et": zz(d)}).wait_recv()
    total = sp[0]
    for i in range(1, NZ):
        total = total + sp[i]
    stot[...] = total.reshape(NY, 1, 128)

    def send_scores(d, carry):
        score_to(lax.rem(e + d, NE)).start()
        return carry

    lax.fori_loop(1, NE, send_scores, 0)
    keep = [
        pltpu.make_async_copy(rsend.at[y, x, c], back.at[e], lsem.at[0]),
        pltpu.make_async_copy(stot.at[y], sback.at[e], lsem.at[1]),
        pltpu.make_async_copy(wsend.at[0, z], gg_ref.at[:, pl.ds(z * W, W)], lsem.at[2]),
        pltpu.make_async_copy(wsend.at[1, z], ug_ref.at[:, pl.ds(z * W, W)], lsem.at[3]),
    ]
    for k in keep:
        k.start()

    hs = jnp.concatenate([hsp[b] for b in range(NY)], axis=1)
    for f in range(NZ):
        rows = row_grad[:, :, f * W : (f + 1) * W].reshape(1024, W)
        dg_ref[:, f * W : (f + 1) * W] = dot(hs, rows).astype(BF)

    ids = ids_ref[...]
    row_e = lax.broadcasted_iota(jnp.int32, (NE, TOK), 0)
    names = jnp.zeros((NE, TOK), F32)
    for k in range(TOP):
        names += (ids[k : k + 1, :] == row_e).astype(F32)
    ti = lax.broadcasted_iota(jnp.int32, (TOK, TOK), 0)
    tj = lax.broadcasted_iota(jnp.int32, (TOK, TOK), 1)
    rank = dot(names.astype(BF), (ti < tj).astype(F32).astype(BF))
    rank = jnp.where(names > 0, rank, -1.0)
    ei = lax.broadcasted_iota(jnp.int32, (1024, NE), 0)
    ej = lax.broadcasted_iota(jnp.int32, (1024, NE), 1)
    spread = (ei // 16 == ej).astype(F32).astype(BF)
    slot = lax.rem(lax.broadcasted_iota(jnp.int32, (1024, TOK), 0), 16).astype(F32)
    gather = (dot(spread, rank.astype(BF)) == slot).astype(F32).astype(BF)

    for k in keep:
        k.wait()

    def wait_back(d, carry):
        t = lax.rem(e + d, NE)
        rows_from(t).wait_recv()
        score_from(t).wait_recv()
        return carry

    lax.fori_loop(1, NE, wait_back, 0)
    tg_ref[...] = dot(gather, back[...].reshape(1024, W), ((0,), (0,))).astype(BF)
    li = lax.broadcasted_iota(jnp.int32, (16, 128), 0)
    lj = lax.broadcasted_iota(jnp.int32, (16, 128), 1)
    mine = (lj == x * 32 + c * 16 + li).astype(F32)
    slots = dot(sback[...].reshape(NE, 128), mine, ((1,), (1,)), lax.Precision.HIGHEST)
    value = jnp.zeros((NE, TOK), F32)
    for j in range(16):
        value += jnp.where(rank == j, slots[:, j : j + 1], 0.0)
    for k in range(TOP):
        sg_ref[k : k + 1, :] = jnp.sum(
            jnp.where(ids[k : k + 1, :] == row_e, value, 0.0), axis=0, keepdims=True
        )

    for k in wout:
        k.wait_recv()
    for k in pend:
        k.wait_send()

    def wait_sent(d, carry):
        t = lax.rem(e + d, NE)
        rows_to(t).wait_send()
        score_to(t).wait_send()
        return carry

    lax.fori_loop(1, NE, wait_sent, 0)


def publish(*refs):
    for i in range(5):
        refs[5 + i][...] = refs[i][...]


def body(
    out_grad, gate_scores, expert_ids, routed_rows, gate_pre, up_pre,
    gate_weight, up_weight, down_weight,
):
    vmem = pl.BlockSpec(memory_space=pltpu.VMEM)
    hbm = pl.BlockSpec(memory_space=pl.ANY)
    dma = pltpu.SemaphoreType.DMA
    outs = pl.pallas_call(
        kernel,
        out_shape=(
            jax.ShapeDtypeStruct((TOK, W), BF),
            jax.ShapeDtypeStruct((TOP, TOK), F32),
            jax.ShapeDtypeStruct((FZ, D), BF),
            jax.ShapeDtypeStruct((FZ, D), BF),
            jax.ShapeDtypeStruct((FZ, D), BF),
        ),
        in_specs=[hbm, vmem, vmem] + [hbm] * 6,
        out_specs=(vmem,) * 5,
        scratch_shapes=[
            pltpu.VMEM((NY, NX, NC, NR, W), BF),
            pltpu.VMEM((2, NZ, FZ, W), BF),
            pltpu.VMEM((NY, NX, 32, W), BF),
            pltpu.VMEM((FZ, 1024), BF),
            pltpu.VMEM((FZ, 1024), BF),
            pltpu.VMEM((FZ, D), BF),
            pltpu.VMEM((NY, 2 * FZ, 128), BF),
            pltpu.VMEM((NY, 128, D), BF),
            pltpu.VMEM((NY, FZ, 128), BF),
            pltpu.VMEM((NY, NZ, 2 * FZ, 128), BF),
            pltpu.VMEM((NZ, NY, 128), F32),
            pltpu.VMEM((NY, 1, 128), F32),
            pltpu.VMEM((2, FF, W), F32),
            pltpu.VMEM((2, NZ, FZ, W), BF),
            pltpu.VMEM((NY, NX, NC, 16, W), BF),
            pltpu.VMEM((NE, 16, W), BF),
            pltpu.VMEM((NE, 1, 128), F32),
            dma((14,)),
            dma((8,)), dma((8,)),
            dma((2, 8)), dma((2, 8)),
            dma((2, 2, 2)), dma((2, 2, 2)),
            dma((2, 5)), dma((2, 5)),
            dma((2, 8, 3)), dma((2, 8, 3)),
            dma((2, 3)), dma((2, 3)),
            dma((2, 4, 5)), dma((2, 4, 5)),
            dma((2, 8)), dma((2, 8)),
            dma((2, 8, 5)), dma((2, 8, 5)),
            dma((8,)), dma((8,)),
            dma((2, 8)), dma((2, 8)),
            dma((NE,)), dma((NE,)),
            dma((NE,)), dma((NE,)),
        ],
        compiler_params=pltpu.CompilerParams(
            collective_id=0, has_side_effects=True, vmem_limit_bytes=56 << 20
        ),
        name="expert_backward",
    )(
        out_grad, expert_ids.T, gate_scores.T, routed_rows.reshape(NX, NY, 32, W),
        gate_pre.reshape(FZ, 1024), up_pre.reshape(FZ, 1024),
        gate_weight.reshape(FZ, D), up_weight.reshape(FZ, D), down_weight.reshape(FZ, D),
    )
    outs = pl.pallas_call(
        publish,
        out_shape=tuple(jax.ShapeDtypeStruct(o.shape, o.dtype) for o in outs),
        in_specs=[vmem] * 5,
        out_specs=(vmem,) * 5,
        name="publish",
    )(*outs)
    token_grad, score_grad, gate_out, up_out, down_out = outs
    return token_grad, score_grad.T, gate_out[None], up_out[None], down_out[None]


def solution(mesh):
    return jax.shard_map(
        body,
        mesh=mesh,
        in_specs=(
            P("exp", "et"), P("exp", None), P("exp", None), P("exp", None, "et"),
            P("exp", "et", None), P("exp", "et", None), P("exp", "et", None),
            P("exp", "et", None), P("exp", "et", None),
        ),
        out_specs=(
            P("exp", "et"), P("exp", None), P("exp", "et", None), P("exp", "et", None),
            P("exp", "et", None),
        ),
        check_vma=False,
    )
```

time: 149 us -> 126 us (0.85)
  Pallas kernels: 140 us -> 125 us
  local copies, waits for them, and re-layouts: 7.23 us -> 0 us
    pallas_call x1, Pallas kernels: 140 us -> 123 us  [body(): pl.pallas_call(kernel, out_shape=(jax.ShapeDtypeStruct((TOK, W), BF), jax...]
    unnamed x16 -> x0, local copies, waits for them, and re-layouts: 7.13 us -> none
    pallas_call x0 -> x1, Pallas kernels: none -> 2.3 us  [body(): pl.pallas_call(publish, out_shape=tuple((jax.ShapeDtypeStruct(o.shape, o....]
where the time goes in v2:
time: 126 us
  Pallas kernels  125 us (99%)
    pallas_call x1, Pallas kernels, body(): pl.pallas_call(kernel, out_shape=(jax.ShapeDtypeStruct((TOK, W), BF), jax...  123 us

profile of v2, /device:TPU:1, one launch (start us, length us, event | category | flops | bytes accessed | tf_op | source)
XLA Modules:
  0.0 126.0 jit_solution(11946282176111991504)
XLA Ops:
  0.6 123.1 %expert_backward.1 = (bf16[64,256]{1,0:T(8,128)(2,1)}, f32[8,64]{1,0:T(8,128)}, bf16[96,2048]{1,0:T(8,128)(2,1)}, bf16[96,2048]{1,0:T(8,128)(2,1)}, bf16[96,2048]{1,0:T(8,128)(2,1)}) custom-call(bf16[64,256]{1,0:T(8,128)(2,1)} %x_ref.1, s32[8,64]{1,0:T(8,128)} %bitcast.18, f32[8,64]{1,0:T(8,128)} %bitcast.19, bf16[4,8,32,256]{3,2,1,0:T(8,128)(2,1)} %bitcast.12, ...), custom_call_target="tpu_custom_call" | custom-call | tf_op jit(solution)/shard_map/expert_backward/pallas_call | solution.py:569
  123.7 2.3 %publish.1 = (bf16[64,256]{1,0:T(8,128)(2,1)}, f32[8,64]{1,0:T(8,128)}, bf16[96,2048]{1,0:T(8,128)(2,1)}, bf16[96,2048]{1,0:T(8,128)(2,1)}, bf16[96,2048]{1,0:T(8,128)(2,1)}) custom-call(bf16[64,256]{1,0:T(8,128)(2,1)} %get-tuple-element.15.refs_0_, f32[8,64]{1,0:T(8,128)} %get-tuple-element.16.refs_1_, bf16[96,2048]{1,0:T(8,128)(2,1)} %get-tuple-element.17.refs_2_, ...), custom_call_target="tpu_custom_call" | custom-call | tf_op jit(solution)/shard_map/publish/pallas_call | solution.py:622

commit v3 on v2

--- a/solution.py
+++ b/solution.py
@@ -19,7 +19,7 @@
 RB = (320, 208)
 RBH = ((320, 96), (416, 112))
 DIRS = (0, 1)
-STEPPED = (0, 1, -1, 2, -2, 3, -3, 4)
+RINGED = (0, 1, -1, 2, -2)
 
 
 def dot(a, b, dims=((1,), (0,)), precision=None):
@@ -38,7 +38,7 @@
 def kernel(
     x_ref, ids_ref, score_ref, rr_ref, gp_hbm, up_hbm, gw_ref, uw_ref, dw_hbm,
     tg_ref, sg_ref, gg_ref, ug_ref, dg_ref,
-    tok, wc, rrp, gp_ref, up_ref, dw_ref, gup, row_grad, hsp, gfull, sp, stot, acc, wsend, rsend, back, sback,
+    tok, wc, rrp, gp_ref, up_ref, dw_ref, gup, row_grad, hsp, gfull, sp, stot, acc, wsend, down, rsend, back, sback,
     lsem, zs, zr, ws, wr, fhs, fhr, ays, ayr, axs, axr, bxs, bxr, bys, byr, prs, prr,
     czs, czr, sps, spr, gs, gr, rs, rr_sem, ss, sr,
 ):
@@ -164,8 +164,7 @@
         return remote(sl, sl, prs.at[i, g % 8], prr.at[i, g % 8], at_xy(0, 0, 1 - c))
 
     def c_z(d, g, s):
-        relayed = s == 2 and g in STEPPED
-        held = 1 if relayed else (0 if s < 3 else 2)
+        held = 2 if s == 4 and g not in RINGED else s - 1
         sl = gfull.at[yy(g), zz(sgn(d) * held)]
         if s == 4:
             sl = sl.at[pl.ds(d * FZ, FZ)]
@@ -215,9 +214,8 @@
         gfull[b, z, 0:FZ] = (hg * up * sig * (1.0 + gate * (1.0 - sig))).astype(BF)
         gfull[b, z, FZ : 2 * FZ] = (hg * silu).astype(BF)
         hsp[b] = (hidden * srow).astype(BF)
-        for s in (1,) if g in STEPPED else (2, 1):
-            for d in DIRS:
-                go(c_z(d, g, s))
+        for d in DIRS:
+            go(c_z(d, g, 1))
 
     def step(g):
         for d in DIRS:
@@ -227,11 +225,16 @@
     def relay(g):
         for d in DIRS:
             c_z(d, g, 2).wait_recv()
-            for s in (3, 4):
+            for s in (3,) if g in RINGED else (3, 4):
                 go(c_z(d, g, s))
 
+    def last(g):
+        for d in DIRS:
+            c_z(d, g, 3).wait_recv()
+            go(c_z(d, g, 4))
+
     def collect(g):
-        for s in (3, 4) if g in STEPPED else (1, 3, 4):
+        for s in (4,) if g in RINGED else (3, 4):
             for d in DIRS:
                 c_z(d, g, s).wait_recv()
 
@@ -336,84 +339,16 @@
 
     comp = compute
     plan = [
-        (bx1,),
-        (ay, 1),
-        (ax0, 1),
-        (ax0, -1),
-        (bx2,),
-        (pb, 0),
-        (ax1, 0),
-        (ay, 2),
-        (ax0, 2),
-        (ax0, -2),
-        (by, 0, 1),
-        (by, 1, 1),
-        (fin, 0),
-        (ax1, 1),
-        (ay, 3),
-        (by, -1, 1),
-        (by, 2, 1),
-        (pb, 1),
-        (pb, -1),
-        (comp, 0),
-        (ax1, -1),
-        (ax0, 3),
-        (ax0, -3),
-        (by, 0, 2),
-        (fin, 1),
-        (ay, 4),
-        (by, 1, 2),
-        (ax1, 2),
-        (comp, 1),
-        (step, 0),
-        (by, -1, 2),
-        (ax0, 4),
-        (fin, -1),
-        (by, 2, 2),
-        (pb, 2),
-        (pb, -2),
-        (comp, -1),
-        (relay, 0),
-        (step, 1),
-        (ax1, -2),
-        (by, 0, 3),
-        (fin, 2),
-        (by, 1, 3),
-        (ax1, 3),
-        (comp, 2),
-        (relay, 1),
-        (step, -1),
-        (by, -1, 3),
-        (fin, -2),
-        (by, 2, 3),
-        (pb, 3),
-        (pb, -3),
-        (comp, -2),
-        (take, 0),
-        (relay, -1),
-        (step, 2),
-        (ax1, -3),
-        (by, 0, 4),
-        (fin, 3),
-        (ax1, 4),
-        (by, 1, 4),
-        (comp, 3),
-        (take, 1),
-        (relay, 2),
-        (step, -2),
-        (by, -1, 4),
-        (by, 2, 4),
-        (pb, 4),
-        (fin, -3),
-        (comp, -3),
-        (take, -1),
-        (relay, -2),
-        (step, 3),
-        (fin, 4),
-        (comp, 4),
-        (take, 2),
-        (relay, 3),
-        (step, -3),
+        (bx1,), (ay, 1), (ax0, 1), (ax0, -1), (bx2,), (pb, 0), (ax1, 0), (ay, 2), (ax0, 2),
+        (ax0, -2), (by, 0, 1), (by, 1, 1), (fin, 0), (ax1, 1), (ay, 3), (by, -1, 1), (by, 2, 1),
+        (pb, 1), (pb, -1), (comp, 0), (ax1, -1), (ax0, 3), (ax0, -3), (by, 0, 2), (fin, 1),
+        (ay, 4), (by, 1, 2), (ax1, 2), (comp, 1), (step, 0), (by, -1, 2), (ax0, 4), (fin, -1),
+        (by, 2, 2), (pb, 2), (pb, -2), (comp, -1), (step, 1), (ax1, -2), (by, 0, 3), (fin, 2),
+        (by, 1, 3), (ax1, 3), (comp, 2), (relay, 0), (step, -1), (by, -1, 3), (fin, -2),
+        (by, 2, 3), (pb, 3), (pb, -3), (comp, -2), (last, 0), (relay, 1), (step, 2), (ax1, -3),
+        (by, 0, 4), (fin, 3), (ax1, 4), (by, 1, 4), (comp, 3), (last, 1), (relay, -1), (step, -2),
+        (by, -1, 4), (by, 2, 4), (pb, 4), (fin, -3), (comp, -3), (take, 0), (last, -1),
+        (relay, 2), (step, 3), (fin, 4), (comp, 4), (take, 1), (last, 2), (relay, -2), (step, -3),
     ]
     for event, *given in plan:
         event(*given)
@@ -450,12 +385,22 @@
     step(4)
     if unsent:
         send_rows(unsent.pop(0))
+    last(-2)
+    if unsent:
+        send_rows(unsent.pop(0))
+    relay(3)
+    if unsent:
+        send_rows(unsent.pop(0))
     relay(-3)
     if unsent:
         send_rows(unsent.pop(0))
     relay(4)
     if unsent:
         send_rows(unsent.pop(0))
+    take(-1)
+    send_rows(unsent.pop(0))
+    take(2)
+    send_rows(unsent.pop(0))
     take(-2)
     send_rows(unsent.pop(0))
     take(3)
@@ -500,7 +445,9 @@
     hs = jnp.concatenate([hsp[b] for b in range(NY)], axis=1)
     for f in range(NZ):
         rows = row_grad[:, :, f * W : (f + 1) * W].reshape(1024, W)
-        dg_ref[:, f * W : (f + 1) * W] = dot(hs, rows).astype(BF)
+        down[:, f * W : (f + 1) * W] = dot(hs, rows).astype(BF)
+    out_down = pltpu.make_async_copy(down, dg_ref, lsem.at[4])
+    out_down.start()
 
     ids = ids_ref[...]
     row_e = lax.broadcasted_iota(jnp.int32, (NE, TOK), 0)
@@ -540,6 +487,7 @@
             jnp.where(ids[k : k + 1, :] == row_e, value, 0.0), axis=0, keepdims=True
         )
 
+    out_down.wait()
     for k in wout:
         k.wait_recv()
     for k in pend:
@@ -576,7 +524,7 @@
             jax.ShapeDtypeStruct((FZ, D), BF),
         ),
         in_specs=[hbm, vmem, vmem] + [hbm] * 6,
-        out_specs=(vmem,) * 5,
+        out_specs=(vmem, vmem, hbm, hbm, hbm),
         scratch_shapes=[
             pltpu.VMEM((NY, NX, NC, NR, W), BF),
             pltpu.VMEM((2, NZ, FZ, W), BF),
@@ -592,6 +540,7 @@
             pltpu.VMEM((NY, 1, 128), F32),
             pltpu.VMEM((2, FF, W), F32),
             pltpu.VMEM((2, NZ, FZ, W), BF),
+            pltpu.VMEM((FZ, D), BF),
             pltpu.VMEM((NY, NX, NC, 16, W), BF),
             pltpu.VMEM((NE, 16, W), BF),
             pltpu.VMEM((NE, 1, 128), F32),

time: 126 us -> 122 us (0.968)
  Pallas kernels: 125 us -> 121 us
    pallas_call x1, Pallas kernels: 123 us -> 119 us  [body(): pl.pallas_call(kernel, out_shape=(jax.ShapeDtypeStruct((TOK, W), BF), jax...]
where the time goes in v3:
time: 122 us
  Pallas kernels  121 us (99%)
    pallas_call x1, Pallas kernels, body(): pl.pallas_call(kernel, out_shape=(jax.ShapeDtypeStruct((TOK, W), BF), jax...  119 us

profile of v3, /device:TPU:1, one launch (start us, length us, event | category | flops | bytes accessed | tf_op | source)
XLA Modules:
  0.0 121.9 jit_solution(7541481023292439281)
XLA Ops:
  0.6 119.0 %expert_backward.1 = (bf16[64,256]{1,0:T(8,128)(2,1)}, f32[8,64]{1,0:T(8,128)}, bf16[96,2048]{1,0:T(8,128)(2,1)}, bf16[96,2048]{1,0:T(8,128)(2,1)}, bf16[96,2048]{1,0:T(8,128)(2,1)}) custom-call(bf16[64,256]{1,0:T(8,128)(2,1)} %x_ref.1, s32[8,64]{1,0:T(8,128)} %bitcast.18, f32[8,64]{1,0:T(8,128)} %bitcast.19, bf16[4,8,32,256]{3,2,1,0:T(8,128)(2,1)} %bitcast.12, ...), custom_call_target="tpu_custom_call" | custom-call | tf_op jit(solution)/shard_map/expert_backward/pallas_call | solution.py:517
  119.6 2.3 %publish.1 = (bf16[64,256]{1,0:T(8,128)(2,1)}, f32[8,64]{1,0:T(8,128)}, bf16[96,2048]{1,0:T(8,128)(2,1)}, bf16[96,2048]{1,0:T(8,128)(2,1)}, bf16[96,2048]{1,0:T(8,128)(2,1)}) custom-call(bf16[64,256]{1,0:T(8,128)(2,1)} %get-tuple-element.15.refs_0_, f32[8,64]{1,0:T(8,128)} %get-tuple-element.16.refs_1_, bf16[96,2048]{1,0:T(8,128)(2,1)} %get-tuple-element.17.refs_2_, ...), custom_call_target="tpu_custom_call" | custom-call | tf_op jit(solution)/shard_map/publish/pallas_call | solution.py:571

commit v4 on v3

--- a/solution.py
+++ b/solution.py
@@ -19,7 +19,7 @@
 RB = (320, 208)
 RBH = ((320, 96), (416, 112))
 DIRS = (0, 1)
-RINGED = (0, 1, -1, 2, -2)
+RINGED = (0, 1, -1, 2, -2, 3)
 
 
 def dot(a, b, dims=((1,), (0,)), precision=None):
@@ -385,9 +385,6 @@
     step(4)
     if unsent:
         send_rows(unsent.pop(0))
-    last(-2)
-    if unsent:
-        send_rows(unsent.pop(0))
     relay(3)
     if unsent:
         send_rows(unsent.pop(0))
@@ -395,6 +392,12 @@
     if unsent:
         send_rows(unsent.pop(0))
     relay(4)
+    if unsent:
+        send_rows(unsent.pop(0))
+    last(-2)
+    if unsent:
+        send_rows(unsent.pop(0))
+    last(3)
     if unsent:
         send_rows(unsent.pop(0))
     take(-1)

time: 122 us -> 125 us (1.025)
  Pallas kernels: 121 us -> 124 us
    pallas_call x1, Pallas kernels: 119 us -> 122 us  [body(): pl.pallas_call(kernel, out_shape=(jax.ShapeDtypeStruct((TOK, W), BF), jax...]
where the time goes in v4:
time: 125 us
  Pallas kernels  124 us (99%)
    pallas_call x1, Pallas kernels, body(): pl.pallas_call(kernel, out_shape=(jax.ShapeDtypeStruct((TOK, W), BF), jax...  122 us

profile of v4, /device:TPU:1, one launch (start us, length us, event | category | flops | bytes accessed | tf_op | source)
XLA Modules:
  0.0 124.6 jit_solution(14380786263593446410)
XLA Ops:
  0.6 121.7 %expert_backward.1 = (bf16[64,256]{1,0:T(8,128)(2,1)}, f32[8,64]{1,0:T(8,128)}, bf16[96,2048]{1,0:T(8,128)(2,1)}, bf16[96,2048]{1,0:T(8,128)(2,1)}, bf16[96,2048]{1,0:T(8,128)(2,1)}) custom-call(bf16[64,256]{1,0:T(8,128)(2,1)} %x_ref.1, s32[8,64]{1,0:T(8,128)} %bitcast.18, f32[8,64]{1,0:T(8,128)} %bitcast.19, bf16[4,8,32,256]{3,2,1,0:T(8,128)(2,1)} %bitcast.12, ...), custom_call_target="tpu_custom_call" | custom-call | tf_op jit(solution)/shard_map/expert_backward/pallas_call | solution.py:520
  122.3 2.3 %publish.1 = (bf16[64,256]{1,0:T(8,128)(2,1)}, f32[8,64]{1,0:T(8,128)}, bf16[96,2048]{1,0:T(8,128)(2,1)}, bf16[96,2048]{1,0:T(8,128)(2,1)}, bf16[96,2048]{1,0:T(8,128)(2,1)}) custom-call(bf16[64,256]{1,0:T(8,128)(2,1)} %get-tuple-element.15.refs_0_, f32[8,64]{1,0:T(8,128)} %get-tuple-element.16.refs_1_, bf16[96,2048]{1,0:T(8,128)(2,1)} %get-tuple-element.17.refs_2_, ...), custom_call_target="tpu_custom_call" | custom-call | tf_op jit(solution)/shard_map/publish/pallas_call | solution.py:574
